TPU v7x, 32 devices: a whole 2x2x4 slice. The times are simulated.
32 devices in a mesh: dp: 8 (over z, x), seq: 4 (over y, core).
Axes of the slice: x: 2, y: 2, z: 4, core: 2. Of those that a mesh axis runs over, the one named last changes fastest.
Arguments:
- tokens: float32 [8192, 384], P(('dp', 'seq')), may hold values from -6 to 6
- class_tokens: float32 [32, 384], P('dp'), may hold values from -6 to 6
- cot_patch: float32 [8192, 384], P(('dp', 'seq')), may hold values from -6 to 6
- cot_class: float32 [32, 384], P('dp'), may hold values from -6 to 6
- lengths: int32 [8, 4], P('dp'), may hold values from 64 to 832, as said below
- matrices: float32 [2, 3, 384, 1536], replicated, may hold values from -0.3125 to 0.3125
- matrices_moment1: float32 [2, 3, 384, 1536], P(None, None, 'dp'), may hold values from -0.00035029993 to 0.00035029993
- matrices_moment2: float32 [2, 3, 384, 1536], P(None, None, 'dp'), may hold values from 2.8170347e-10 to 1.1268139e-09
- matrices_ema: float32 [2, 3, 384, 1536], P(None, None, 'dp'), may hold values from -0.3125 to 0.3125
- vectors: float32 [28, 384], replicated, may hold values from -1 to 3
- vectors_moment1: float32 [28, 384], P(None, 'dp'), may hold values from -0.0014011997 to 0.0014011997
- vectors_moment2: float32 [28, 384], P(None, 'dp'), may hold values from 4.5072555e-09 to 1.8029022e-08
- vectors_ema: float32 [28, 384], P(None, 'dp'), may hold values from 0.5 to 1.5
- talking: float32 [8, 17], replicated, may hold values from -1 to 2
- talking_moment1: float32 [8, 17], replicated, may hold values from -0.0035029992 to 0.0035029992
- talking_moment2: float32 [8, 17], replicated, may hold values from 2.8170348e-08 to 1.1268139e-07
- talking_ema: float32 [8, 17], replicated, may hold values from -3 to 3
Outputs:
- patch_out: float32 [8192, 384], P(('dp', 'seq'))
- class_out: float32 [32, 384], P('dp')
- grad_tokens: float32 [8192, 384], P(('dp', 'seq'))
- grad_class: float32 [32, 384], P('dp')
- clip_norm: float32 [], replicated
- matrices_new: float32 [2, 3, 384, 1536], P(None, None, 'dp')
- matrices_first: float32 [2, 3, 384, 1536], P(None, None, 'dp')
- matrices_second: float32 [2, 3, 384, 1536], P(None, None, 'dp')
- matrices_average: float32 [2, 3, 384, 1536], P(None, None, 'dp')
- vectors_new: float32 [28, 384], P(None, 'dp')
- vectors_first: float32 [28, 384], P(None, 'dp')
- vectors_second: float32 [28, 384], P(None, 'dp')
- vectors_average: float32 [28, 384], P(None, 'dp')
- talking_new: float32 [8, 17], replicated
- talking_first: float32 [8, 17], replicated
- talking_second: float32 [8, 17], replicated
- talking_average: float32 [8, 17], replicated
Inputs may be any that keep to these rules, and one draw needn't show every extreme that they name: In every data group the 4 lengths sum to 1024; one image of each group, neither the first nor the last and in a drawn place, begins within the first 256 positions of the group and ends within its last 256.
All inputs are finite; a program needn't handle non-finite values.
Results may differ from a plain program's by a relative error of at most 0.0003.
Values sent between devices are 32-bit elements; how exact they have to be, the bound alone decides.
No kernel may reach another device: no remote copies, remote signals or barrier semaphores. Data moves between devices by JAX's collectives and lax.ppermute only.
A program may use at most 256 MiB of HBM per device.

v0:
```python
import jax
import jax.numpy as jnp
from jax import lax
from jax.sharding import PartitionSpec as P

STEP = 10


EPS_NORM = 1e-06
MASKED = -1e30
LR_MATRIX = 0.05
LR_VECTOR = 0.1
LR_TALKING = 0.2
BETA_ONE = 0.9
BETA_TWO = 0.999
ADAM_EPS = 1e-08
WEIGHT_DECAY = 0.05
EMA_RATE = 0.9
CLIP_NORM = 1.0
HIGHEST = lax.Precision.HIGHEST


def merged(value, axis, join):
    pieces = jax.tree.map(lambda part: lax.all_gather(part, axis), value)
    head = jax.tree.map(lambda part: part[0], pieces)
    tail = jax.tree.map(lambda part: part[1:], pieces)
    total, _ = lax.scan(lambda total, slab: (join(total, slab), None), head, tail)
    return total


def matmul(left, right):
    return jnp.dot(left, right, precision=HIGHEST, preferred_element_type=jnp.float32)


def layer_norm(values, gain_row, shift_row):
    average = jnp.mean(values, axis=-1, keepdims=True)
    centered = values - average
    variance = jnp.mean(centered * centered, axis=-1, keepdims=True)
    return centered * lax.rsqrt(variance + EPS_NORM) * gain_row + shift_row


def project_all(inputs, mats, vecs):
    model_width = inputs.shape[1]
    normed = layer_norm(inputs, vecs[0], vecs[1])
    query = matmul(normed, mats[0][:, :model_width]) + vecs[2]
    keys = matmul(normed, mats[0][:, model_width : 2 * model_width])
    values = matmul(normed, mats[0][:, 2 * model_width : 3 * model_width]) + vecs[3]
    return (query, keys, values)


def project_query(inputs, mats, vecs):
    model_width = inputs.shape[1]
    normed = layer_norm(inputs, vecs[0], vecs[1])
    query = matmul(normed, mats[0][:, :model_width]) + vecs[2]
    return (normed, query)


def project_keys(inputs, mats, vecs):
    model_width = inputs.shape[1]
    normed = layer_norm(inputs, vecs[0], vecs[1])
    keys = matmul(normed, mats[0][:, model_width : 2 * model_width])
    values = matmul(normed, mats[0][:, 2 * model_width : 3 * model_width]) + vecs[3]
    return (keys, values)


def block_tail(inputs, attended, mats, vecs):
    model_width = inputs.shape[1]
    mixed_rows = inputs + vecs[5] * (matmul(attended, mats[0][:, 3 * model_width :]) + vecs[4])
    normed = layer_norm(mixed_rows, vecs[6], vecs[7])
    hidden = jax.nn.gelu(matmul(normed, mats[1]) + vecs[8:12].reshape(-1), approximate=False)
    output_rows = jnp.einsum("nf,df->nd", hidden, mats[2], precision=HIGHEST)
    return mixed_rows + vecs[13] * (output_rows + vecs[12])


def segment_ids(positions, image_lengths):
    image_ends = jnp.cumsum(image_lengths)
    return jnp.sum((positions[:, None] >= image_ends[None, :]).astype(jnp.int32), axis=1)


def local_fold(step_fn, initial, stacked, row_count):
    pieces_count = stacked[0].shape[0] // row_count
    reshaped = tuple(
        (member.reshape(pieces_count, row_count, member.shape[1]) for member in stacked)
    )

    def advance(running, element):
        return (step_fn(running, element[1], element[0] * row_count), None)

    numbers = jnp.arange(pieces_count)
    return lax.scan(advance, initial, (numbers, reshaped))[0]


def combine_partial(earlier, later):
    new_top = jnp.maximum(earlier[0], later[0])
    first_scale = jnp.exp(earlier[0] - new_top)
    second_scale = jnp.exp(later[0] - new_top)
    summed = earlier[1] * first_scale + later[1] * second_scale
    valued = earlier[2] * first_scale[..., None] + later[2] * second_scale[..., None]
    return (new_top, summed, valued)


def adam_step(weight, gradient, moment1, moment2, rate, decay):
    first = BETA_ONE * moment1 + (1.0 - BETA_ONE) * gradient
    second = BETA_TWO * moment2 + (1.0 - BETA_TWO) * gradient * gradient
    first_hat = first / (1.0 - BETA_ONE**STEP)
    second_hat = second / (1.0 - BETA_TWO**STEP)
    updated = weight - rate * (first_hat / (jnp.sqrt(second_hat) + ADAM_EPS) + decay * weight)
    return (updated, first, second)


def on_device(
    tokens,
    class_tokens,
    cot_patch,
    cot_class,
    lengths,
    matrices,
    matrices_moment1,
    matrices_moment2,
    matrices_ema,
    vectors,
    vectors_moment1,
    vectors_moment2,
    vectors_ema,
    talking,
    talking_moment1,
    talking_moment2,
    talking_ema,
):
    tok_rows, model_width = tokens.shape
    images = class_tokens.shape[0]
    head_count = talking.shape[0]
    head_size = model_width // head_count
    score_scale = head_size ** (-0.5)
    seq_index = lax.axis_index("seq")
    image_lengths = lengths[0]

    def segment_at(offset, piece_rows):
        return segment_ids(offset + jnp.arange(piece_rows), image_lengths)

    own_segment = segment_at(seq_index * tok_rows, tok_rows)
    mats_self = matrices[0]
    mats_class = matrices[1]
    vecs_self = vectors[:14]
    vecs_class = vectors[14:]
    pre_mix = talking[:, :head_count]
    post_mix = talking[:, head_count : 2 * head_count]
    post_bias = talking[:, 2 * head_count]
    w_kv = mats_self[0][:, model_width : 3 * model_width]
    kv_bias = jnp.concatenate([jnp.zeros((model_width,), jnp.float32), vecs_self[3]])
    (normed_self, query), pull_self = jax.vjp(project_query, tokens, mats_self, vecs_self)
    query_split = query.reshape(tok_rows, head_count, head_size)
    sent = matmul(normed_self, w_kv) + kv_bias
    first_rows = sent[:, :model_width]

    def piece_kv(piece):
        return (piece[:, :model_width], piece[:, model_width:])

    def scores_for(key_rows, offset):
        piece_rows = key_rows.shape[0]
        keys_split = key_rows.reshape(piece_rows, head_count, head_size)
        raw_scores = (
            jnp.einsum("ihe,jhe->hij", query_split, keys_split, precision=HIGHEST) * score_scale
        )
        mixed_scores = jnp.einsum("hg,gij->hij", pre_mix, raw_scores, precision=HIGHEST)
        inside = (own_segment[:, None] == segment_at(offset, piece_rows)[None, :])[None]
        return (raw_scores, jnp.where(inside, mixed_scores, MASKED), inside)

    def probabilities_of(masked_scores, inside):
        return jnp.exp(masked_scores - log_sum[..., None]) * inside

    def mixed_weights(probabilities, inside):
        weights = jnp.einsum("hg,gij->hij", post_mix, probabilities, precision=HIGHEST)
        return weights + post_bias[:, None, None] * inside

    running_top = jnp.full((head_count, tok_rows), MASKED, jnp.float32)
    raw_scores, masked_scores, inside = scores_for(
        (lax.all_gather(first_rows, "seq", axis=0, tiled=True),)[0], jnp.int32(0)
    )
    new_top = jnp.maximum(running_top, jnp.max(masked_scores, axis=2))
    exponentials = jnp.exp(masked_scores - new_top[..., None]) * inside
    running_sum = jnp.sum(exponentials, axis=2)
    log_sum = new_top + jnp.log(running_sum)
    key_rows, value_rows = piece_kv((lax.all_gather(sent, "seq", axis=0, tiled=True),)[0])
    raw_scores, masked_scores, inside = scores_for(key_rows, jnp.int32(0))
    weights = mixed_weights(probabilities_of(masked_scores, inside), inside)
    values_split = value_rows.reshape(-1, head_count, head_size)
    attended = jnp.einsum("hij,jhe->ihe", weights, values_split, precision=HIGHEST)
    patch_out, pull_tail = jax.vjp(
        block_tail, tokens, attended.reshape(tok_rows, model_width), mats_self, vecs_self
    )
    (patch_keys, patch_values), pull_keys = jax.vjp(project_keys, patch_out, mats_class, vecs_class)
    (query_cls, keys_cls, values_cls), pull_query = jax.vjp(
        project_all, class_tokens, mats_class, vecs_class
    )
    query_heads = query_cls.reshape(images, head_count, head_size)
    own_keys = keys_cls.reshape(images, head_count, head_size)
    own_values = values_cls.reshape(images, head_count, head_size)
    patch_key_split = patch_keys.reshape(tok_rows, head_count, head_size)
    patch_value_split = patch_values.reshape(tok_rows, head_count, head_size)
    image_ids = jnp.arange(images)
    belong = (own_segment[None, :] == image_ids[:, None])[:, None, :]
    patch_scores = (
        jnp.einsum("ahe,jhe->ahj", query_heads, patch_key_split, precision=HIGHEST) * score_scale
    )
    patch_scores = jnp.where(belong, patch_scores, MASKED)
    own_score = jnp.sum(query_heads * own_keys, axis=2) * score_scale
    local_top = jnp.max(patch_scores, axis=2)
    local_weights = jnp.exp(patch_scores - local_top[..., None]) * belong
    local_values = jnp.einsum("ahj,jhe->ahe", local_weights, patch_value_split, precision=HIGHEST)
    merged_top, merged_sum, merged_values = merged(
        (local_top, jnp.sum(local_weights, axis=2), local_values), "seq", combine_partial
    )
    class_top = jnp.maximum(merged_top, own_score)
    rescale = jnp.exp(merged_top - class_top)
    own_weight = jnp.exp(own_score - class_top)
    class_sum = merged_sum * rescale + own_weight
    class_attended = (
        merged_values * rescale[..., None] + own_weight[..., None] * own_values
    ) / class_sum[..., None]
    class_log = class_top + jnp.log(class_sum)
    class_out, pull_class_tail = jax.vjp(
        block_tail,
        class_tokens,
        class_attended.reshape(images, model_width),
        mats_class,
        vecs_class,
    )
    is_first = (seq_index == 0).astype(jnp.float32)
    grad_class_tail, d_class_attended, mats_class_tail, vecs_class_tail = pull_class_tail(cot_class)
    dout_class = d_class_attended.reshape(images, head_count, head_size)
    class_delta = jnp.sum(dout_class * class_attended, axis=2)
    patch_probs = jnp.exp(patch_scores - class_log[..., None]) * belong
    patch_dprobs = jnp.einsum("ahe,jhe->ahj", dout_class, patch_value_split, precision=HIGHEST)
    patch_dscores = patch_probs * (patch_dprobs - class_delta[..., None]) * score_scale
    d_patch_keys = jnp.einsum(
        "ahj,ahe->jhe", patch_dscores, query_heads, precision=HIGHEST
    ).reshape(tok_rows, model_width)
    d_patch_values = jnp.einsum("ahj,ahe->jhe", patch_probs, dout_class, precision=HIGHEST).reshape(
        tok_rows, model_width
    )
    d_query_local = jnp.einsum("ahj,jhe->ahe", patch_dscores, patch_key_split, precision=HIGHEST)
    own_prob = jnp.exp(own_score - class_log)
    own_dscore = own_prob * (jnp.sum(dout_class * own_values, axis=2) - class_delta) * score_scale
    d_own_keys = (own_dscore[..., None] * query_heads).reshape(images, model_width)
    d_own_values = (own_prob[..., None] * dout_class).reshape(images, model_width)
    d_query_terms = d_query_local + is_first * own_dscore[..., None] * own_keys
    d_query_cls = lax.psum(d_query_terms, "seq")
    grad_class_query, mats_class_query, vecs_class_query = pull_query(
        (d_query_cls.reshape(images, model_width), d_own_keys, d_own_values)
    )
    grad_class = grad_class_tail + grad_class_query
    d_patch_class, mats_class_keys, vecs_class_keys = pull_keys((d_patch_keys, d_patch_values))
    grad_tokens_tail, d_attended, mats_self_tail, vecs_self_tail = pull_tail(
        cot_patch + d_patch_class
    )
    gathered = (lax.all_gather(sent, "seq", axis=0, tiled=True),)
    dout_split = d_attended.reshape(tok_rows, head_count, head_size)

    def first_back(running, pieces, offset):
        cross_sums, bias_sums = running
        key_rows, value_rows = piece_kv(pieces[0])
        raw_scores, masked_scores, inside = scores_for(key_rows, offset)
        probabilities = probabilities_of(masked_scores, inside)
        values_split = value_rows.reshape(-1, head_count, head_size)
        d_weights = jnp.einsum("ihe,jhe->hij", dout_split, values_split, precision=HIGHEST) * inside
        cross_sums = cross_sums + jnp.einsum(
            "gij,hij->igh", probabilities, d_weights, precision=HIGHEST
        )
        return (cross_sums, bias_sums + jnp.sum(d_weights, axis=2))

    back_init = (
        jnp.zeros((tok_rows, head_count, head_count), jnp.float32),
        jnp.zeros((head_count, tok_rows), jnp.float32),
    )
    cross_sums, bias_sums = local_fold(first_back, back_init, gathered, tok_rows)
    delta = jnp.einsum("hg,igh->gi", post_mix, cross_sums, precision=HIGHEST)
    grad_post = jnp.einsum("igh->hg", cross_sums)
    grad_bias = jnp.sum(bias_sums, axis=1)

    def second_back(running, element):
        number, pieces = element
        offset = number * tok_rows
        d_query, grad_pre, grad_wkv, grad_kv_bias = running
        key_rows, value_rows = piece_kv(pieces[0])
        raw_scores, masked_scores, inside = scores_for(key_rows, offset)
        keys_split = key_rows.reshape(-1, head_count, head_size)
        values_split = value_rows.reshape(-1, head_count, head_size)
        probabilities = probabilities_of(masked_scores, inside)
        weights = mixed_weights(probabilities, inside)
        d_weights = jnp.einsum("ihe,jhe->hij", dout_split, values_split, precision=HIGHEST) * inside
        d_probs = jnp.einsum("hg,hij->gij", post_mix, d_weights, precision=HIGHEST)
        d_mixed = probabilities * (d_probs - delta[..., None])
        grad_pre = grad_pre + jnp.einsum("hij,gij->hg", d_mixed, raw_scores, precision=HIGHEST)
        d_raw = jnp.einsum("hg,hij->gij", pre_mix, d_mixed, precision=HIGHEST) * score_scale
        d_query = d_query + jnp.einsum("hij,jhe->ihe", d_raw, keys_split, precision=HIGHEST)
        d_keys_piece = jnp.einsum("hij,ihe->jhe", d_raw, query_split, precision=HIGHEST).reshape(
            -1, model_width
        )
        d_values_piece = jnp.einsum("hij,ihe->jhe", weights, dout_split, precision=HIGHEST).reshape(
            -1, model_width
        )
        d_kv_piece = jnp.concatenate([d_keys_piece, d_values_piece], axis=1)
        return ((d_query, grad_pre, grad_wkv, grad_kv_bias), d_kv_piece)

    cycle_count = gathered[0].shape[0] // tok_rows
    stacked = (gathered[0].reshape(cycle_count, tok_rows, gathered[0].shape[1]),)
    second_init = (
        jnp.zeros((tok_rows, head_count, head_size), jnp.float32),
        jnp.zeros((head_count, head_count), jnp.float32),
        jnp.zeros((model_width, 2 * model_width), jnp.float32),
        jnp.zeros((2 * model_width,), jnp.float32),
    )
    (d_query, grad_pre, grad_wkv, grad_kv_bias), back_terms = lax.scan(
        second_back, second_init, (jnp.arange(cycle_count), stacked)
    )
    d_own = (
        lax.psum_scatter(
            back_terms.reshape(-1, back_terms.shape[2]), "seq", scatter_dimension=0, tiled=True
        ),
    )[0]
    d_normed_own = matmul(d_own, w_kv.T)
    grad_wkv = matmul(normed_self.T, d_own)
    grad_kv_bias = jnp.sum(d_own, axis=0)
    grad_tokens_pre, mats_self_pre, vecs_self_pre = pull_self(
        (d_normed_own, d_query.reshape(tok_rows, model_width))
    )
    mats_self_pre = mats_self_pre.at[0, :, model_width : 3 * model_width].add(grad_wkv)
    vecs_self_pre = vecs_self_pre.at[3].add(grad_kv_bias[model_width:])
    grad_tokens = grad_tokens_tail + grad_tokens_pre
    grad_mats = jnp.stack(
        [
            mats_self_tail + mats_self_pre,
            is_first * (mats_class_tail + mats_class_query) + mats_class_keys,
        ]
    )
    grad_vecs = jnp.concatenate(
        [
            vecs_self_tail + vecs_self_pre,
            is_first * (vecs_class_tail + vecs_class_query) + vecs_class_keys,
        ],
        axis=0,
    )
    grad_talk = jnp.concatenate([grad_pre, grad_post, grad_bias[:, None]], axis=1)
    grad_mats, grad_vecs, grad_talk = lax.psum((grad_mats, grad_vecs, grad_talk), "seq")
    mats_share, vecs_share = (
        lax.psum_scatter(grad_mats, "dp", scatter_dimension=2, tiled=True),
        lax.psum_scatter(grad_vecs, "dp", scatter_dimension=1, tiled=True),
    )
    share_squares = jnp.sum(mats_share * mats_share) + jnp.sum(vecs_share * vecs_share)
    grad_talk, share_squares = lax.psum((grad_talk, share_squares), "dp")
    clip_norm = jnp.sqrt(share_squares + jnp.sum(grad_talk * grad_talk))
    factor = jnp.minimum(1.0, CLIP_NORM / clip_norm)
    dp_index = lax.axis_index("dp")
    row_share = mats_share.shape[2]
    column_share = vecs_share.shape[1]
    weight_rows = lax.dynamic_slice_in_dim(matrices, dp_index * row_share, row_share, 2)
    vector_columns = lax.dynamic_slice_in_dim(vectors, dp_index * column_share, column_share, 1)
    matrices_new, matrices_first, matrices_second = adam_step(
        weight_rows,
        mats_share * factor,
        matrices_moment1,
        matrices_moment2,
        LR_MATRIX,
        WEIGHT_DECAY,
    )
    vectors_new, vectors_first, vectors_second = adam_step(
        vector_columns, vecs_share * factor, vectors_moment1, vectors_moment2, LR_VECTOR, 0.0
    )
    talking_new, talking_first, talking_second = adam_step(
        talking, grad_talk * factor, talking_moment1, talking_moment2, LR_TALKING, 0.0
    )
    matrices_average = EMA_RATE * matrices_ema + (1.0 - EMA_RATE) * matrices_new
    vectors_average = EMA_RATE * vectors_ema + (1.0 - EMA_RATE) * vectors_new
    talking_average = EMA_RATE * talking_ema + (1.0 - EMA_RATE) * talking_new
    return (
        patch_out,
        class_out,
        grad_tokens,
        grad_class,
        clip_norm,
        matrices_new,
        matrices_first,
        matrices_second,
        matrices_average,
        vectors_new,
        vectors_first,
        vectors_second,
        vectors_average,
        talking_new,
        talking_first,
        talking_second,
        talking_average,
    )


def solution(mesh):
    placed = (
        P(("dp", "seq"), None),
        P("dp", None),
        P(("dp", "seq"), None),
        P("dp", None),
        P("dp", None),
        P(),
        P(None, None, "dp", None),
        P(None, None, "dp", None),
        P(None, None, "dp", None),
        P(),
        P(None, "dp"),
        P(None, "dp"),
        P(None, "dp"),
        P(),
        P(),
        P(),
        P(),
    )
    return jax.shard_map(
        on_device,
        mesh=mesh,
        in_specs=placed,
        out_specs=(
            P(("dp", "seq"), None),
            P("dp", None),
            P(("dp", "seq"), None),
            P("dp", None),
            P(),
            P(None, None, "dp", None),
            P(None, None, "dp", None),
            P(None, None, "dp", None),
            P(None, None, "dp", None),
            P(None, "dp"),
            P(None, "dp"),
            P(None, "dp"),
            P(None, "dp"),
            P(),
            P(),
            P(),
            P(),
        ),
        check_vma=False,
    )
```

profile of v0, /device:TPU:0, one launch (start us, length us, event | category | flops | bytes accessed | tf_op | source)
XLA Modules:
  0.0 989.4 jit_solution(11668673513583988075)
XLA Ops:
  42.9 7.2 broadcast_multiply_fusion
  50.2 18.0 %bitcast_reduce_fusion = (f32[8,256]{0,1:T(8,128)S(1)}, f32[256,1024,8]{1,2,0:T(8,128)S(1)}) fusion(pred[256,1024]{1,0:T(8,128)(4,1)S(1)} %copy-done.38, f32[8,17]{1,0:T(8,128)S(1)} %copy-done.70, f32[8,256,1024]{2,1,0:T(8,128)S(1)} %broadcast_multiply_fusion), kind=kOutput, calls=%fused_computation.65 | convolution fusion | flops 205518848 | bytes 17048096 | tf_op jit(solution)/shard_map/hg,gij->hij/dot_general | solution.py:165
  77.5 7.2 broadcast_multiply_fusion.1
  84.7 13.8 %fusion.54 = f32[256,1024,8]{1,2,0:T(8,128)} fusion(f32[8,256,1024]{2,1,0:T(8,128)S(1)} %broadcast_multiply_fusion.1, f32[8,17]{1,0:T(8,128)S(1)} %copy-done.70), kind=kOutput, calls=%fused_computation.77 | convolution fusion | flops 201326592 | bytes 16777760 | tf_op jit(solution)/shard_map/hg,gij->hij/dot_general | solution.py:165
  100.3 12.5 %bitcast_add_fusion.1 = f32[8,256,1024]{2,0,1:T(8,128)S(1)} fusion(f32[8]{0:T(128)S(1)} %bitcast.446, f32[256,1024]{1,0:T(8,128)S(1)} %get-tuple-element.807, f32[256,1024,8]{1,2,0:T(8,128)} %fusion.54, f32[8,256]{0,1:T(8,128)} %log_add_fusion, pred[256,1024]{1,0:T(8,128)(4,1)} %get-tuple-element.806, f32[8,17]{1,0:T(8,128)S(1)} %copy-done.70), kind=kOutput, calls=%fused_computation.63 | convolution fusion | flops 211812352 | bytes 19149312 | tf_op jit(solution)/shard_map/hg,gij->hij/dot_general | solution.py:173
  112.9 11.9 %fusion.50 = f32[8,48,256]{2,1,0:T(8,128)S(1)} fusion(f32[1024,8,48]{0,2,1:T(8,128)S(1)} %bitcast.430, f32[8,256,1024]{2,0,1:T(8,128)S(1)} %bitcast_add_fusion.1), kind=kOutput, calls=%fused_computation.73 | convolution fusion | flops 1207959552 | bytes 10354688 | tf_op jit(solution)/shard_map/hij,jhe->ihe/dot_general | solution.py:188
  128.0 7.6 fusion.90
  135.7 6.4 fusion.228
  216.1 103.1 %while.49 = (s32[]{:T(128)}, f32[256,8,8]{2,1,0:T(8,128)}, f32[8,256]{0,1:T(8,128)}, s32[256]{0:T(256)S(1)}, s32[4]{0:T(128)}, /*index=5*/s32[1,4]{1,0:T(1,128)}...) while((s32[]{:T(128)}, f32[256,8,8]{2,1,0:T(8,128)}, ...), condition=%wide.region_31.32_spmd.clone, body=%wide.region_28.31_spmd.clone.sunk | while | flops 708482048 | bytes 29210128 | solution.py:90
  321.9 196.9 %while.50 = (s32[]{:T(128)}, f32[256,8,48]{0,2,1:T(8,128)}, f32[8,8]{1,0:T(8,128)}, f32[4,256,768]{2,1,0:T(8,128)}, f32[4,256,768]{1,2,0:T(8,128)}, /*index=5*/s...) while((s32[]{:T(128)}, f32[256,8,48]{0,2,1:T(8,128)}, ...), condition=%wide.region_34.35_spmd.clone, body=%wide.region_32.34_spmd.clone.sunk | while | flops 1767378048 | bytes 90465888 | solution.py:314
  360.4 6.8 fusion.372
  408.7 6.8 fusion.372
  458.0 6.8 fusion.372
  507.4 6.8 fusion.372
  522.3 10.3 %psum.42 = f32[4,8,48]{2,0,1:T(4,128)S(1)} all-reduce(f32[4,8,48]{2,0,1:T(4,128)S(1)} %fusion.106), channel_id=1, replica_groups=mesh['dp'=8,'seq'=4] {'seq'}, use_global_device_ids=true, to_apply=%region_39.40 | all-reduce | flops 1536 | bytes 12288 | tf_op jit(solution)/shard_map/psum | solution.py:248
  572.5 8.5 scatter-add.6
  581.0 7.0 add_bitcast_fusion.1
  588.0 12.9 %pad_maximum_fusion = f32[2,3,384,1536]{3,2,1,0:T(8,128)} fusion(f32[1,3,384,1536]{3,2,1,0:T(8,128)} %add_bitcast_fusion, f32[1,3,384,1536]{3,2,1,0:T(8,128)} %add_bitcast_fusion.1), kind=kLoop, calls=%fused_computation.62 | loop fusion | flops 3538944 | bytes 28311552 | tf_op jit(solution)/shard_map/stack | solution.py:331
  634.4 197.3 %reduce-scatter.8.cloned.1.call-done = f32[2,3,48,1536]{3,2,1,0:T(8,128)} async-done(((f32[2,3,384,1536]{3,2,1,0:T(8,128)}), f32[2,3,48,1536]{3,2,1,0:T(8,128)}) %reduce-scatter.8.cloned.1.call-update) | async-done | bytes 1769488 | tf_op jit(solution)/shard_map/reduce_scatter | solution.py:347
  833.0 62.9 %reduce-scatter.10.cloned.1.call-done = f32[48,28]{1,0:T(8,128)} async-done(((f32[384,28]{1,0:T(8,128)}), f32[48,28]{1,0:T(8,128)}) %reduce-scatter.10.cloned.1.call-update) | async-done | bytes 5392
  896.7 11.3 %all-reduce.46 = (f32[28,48]{1,0:T(8,128)S(1)}, f32[8,17]{1,0:T(8,128)}) all-reduce(f32[28,48]{1,0:T(8,128)S(1)} %copy.244, f32[8,17]{1,0:T(8,128)S(1)} %pad_maximum_fusion.2), channel_id=1, replica_groups=mesh['dp'=8,'seq'=4] {'seq'}, use_global_device_ids=true, to_apply=%region_71.72 | all-reduce | flops 1480 | bytes 11840 | tf_op jit(solution)/shard_map/psum | solution.py:345
  908.6 34.9 %all-reduce.49.cloned.1.call-done = f32[2,3,48,1536]{3,2,1,0:T(8,128)} async-done(((f32[2,3,48,1536]{3,2,1,0:T(8,128)}), f32[2,3,48,1536]{3,2,1,0:T(8,128)}) %all-reduce.49.cloned.1.call-update) | async-done | bytes 1769488 | tf_op jit(solution)/shard_map/psum | solution.py:345
  947.5 22.2 %all-reduce.45 = (f32[]{:T(128)}, f32[8,17]{1,0:T(8,128)S(1)}) all-reduce(f32[]{:T(128)S(6)} %add.602, f32[8,17]{1,0:T(8,128)} %get-tuple-element.747), channel_id=1, replica_groups=mesh['dp'=8,'seq'=4] {'dp'}, use_global_device_ids=true, to_apply=%region_74.75 | all-reduce | flops 137 | bytes 1096 | tf_op jit(solution)/shard_map/psum | solution.py:351
  974.5 6.7 multiply_add_fusion
  (754 shorter events, 476.7 us)
Async XLA Ops:
  7.2 33.8 %all-gather.10.cloned.1.call-start = ((), (), s32[]{:S(2)}) async-start(), calls=%async_computation.4 | async-start | bytes 1966080 | tf_op jit(solution)/shard_map/all_gather | solution.py:178
  18.5 53.3 %all-gather.8.cloned.1.call-start = ((), (), s32[]{:S(2)}) async-start(), calls=%async_computation.3 | async-start | bytes 3932160 | tf_op jit(solution)/shard_map/all_gather | solution.py:184
  19.2 547.8 %reduce-scatter.6.cloned.1.call-start = ((), (), s32[]{:S(2)}) async-start(), calls=%async_computation.5 | async-start | bytes 3932160 | tf_op jit(solution)/shard_map/reduce_scatter | solution.py:318
  24.7 75.6 %copy-start.130 = (f32[8,1]{0,1:T(1,128)}, f32[8,1]{0,1:T(1,128)S(1)}, u32[]{:S(2)}) copy-start(f32[8,1]{0,1:T(1,128)S(1)} %copy.247) | copy-start | bytes 100
  34.7 119.9 %copy-start.83 = (f32[4,256]{1,0:T(4,128)}, f32[4,256]{1,0:T(4,128)S(1)}, u32[]{:S(2)}) copy-start(f32[4,256]{1,0:T(4,128)S(1)} %get-tuple-element.811) | copy-start | bytes 12292
  127.8 80.6 %copy-start.21 = (f32[256,384]{1,0:T(8,128)}, f32[256,384]{1,0:T(8,128)S(1)}, u32[]{:S(2)}) copy-start(f32[256,384]{1,0:T(8,128)S(1)} %get-tuple-element.788) | copy-start | bytes 1179652
  127.8 80.6 %copy-start.128 = (f32[256]{0:T(256)}, f32[256]{0:T(256)S(1)}, u32[]{:S(2)}) copy-start(f32[256]{0:T(256)S(1)} %broadcast_multiply_fusion.5) | copy-start | bytes 3076
  128.0 80.4 %copy-start.140 = (f32[256]{0:T(256)}, f32[256]{0:T(256)S(1)}, u32[]{:S(2)}) copy-start(f32[256]{0:T(256)S(1)} %fusion.196) | copy-start | bytes 3076
  135.6 61.3 %copy-start.14 = (f32[256,1536]{1,0:T(8,128)}, f32[256,1536]{1,0:T(8,128)S(1)}, u32[]{:S(2)}) copy-start(f32[256,1536]{1,0:T(8,128)S(1)} %get-tuple-element.818) | copy-start | bytes 4718596
  142.1 53.8 %copy-start.11 = (f32[256,384]{1,0:T(8,128)}, f32[256,384]{1,0:T(8,128)S(1)}, u32[]{:S(2)}) copy-start(f32[256,384]{1,0:T(8,128)S(1)} %get-tuple-element.786) | copy-start | bytes 1179652
  142.1 53.8 %copy-start.100 = (f32[256]{0:T(256)}, f32[256]{0:T(256)S(1)}, u32[]{:S(2)}) copy-start(f32[256]{0:T(256)S(1)} %broadcast_multiply_fusion.4) | copy-start | bytes 3076
  142.3 53.5 %copy-start.119 = (f32[256]{0:T(256)}, f32[256]{0:T(256)S(1)}, u32[]{:S(2)}) copy-start(f32[256]{0:T(256)S(1)} %fusion.197) | copy-start | bytes 3076
  519.0 312.8 %reduce-scatter.8.cloned.1.call-start = ((), (), s32[]{:S(2)}) async-start(), calls=%async_computation.6 | async-start | bytes 15925248 | tf_op jit(solution)/shard_map/reduce_scatter | solution.py:347
  600.9 295.0 %reduce-scatter.10.cloned.1.call-start = ((), (), s32[]{:S(2)}) async-start(), calls=%async_computation.8 | async-start | bytes 221184
  633.1 198.6 %copy-start.145 = (f32[256]{0:T(256)S(1)}, f32[256]{0:T(256)}, u32[]{:S(2)}) copy-start(f32[256]{0:T(256)} %copy-done.144) | copy-start | bytes 3076
  633.1 198.6 %copy-start.99 = (f32[256]{0:T(256)S(1)}, f32[256]{0:T(256)}, u32[]{:S(2)}) copy-start(f32[256]{0:T(256)} %copy-done.97) | copy-start | bytes 3076
  633.1 198.6 %copy-start.118 = (f32[256]{0:T(256)S(1)}, f32[256]{0:T(256)}, u32[]{:S(2)}) copy-start(f32[256]{0:T(256)} %copy-done.116) | copy-start | bytes 3076
  633.2 198.9 %copy-start.31 = (f32[256,384]{1,0:T(8,128)S(1)}, f32[256,384]{1,0:T(8,128)}, u32[]{:S(2)}) copy-start(f32[256,384]{1,0:T(8,128)} %copy-done.29) | copy-start | bytes 1179652
  633.3 198.5 %copy-start.49 = (f32[256,384]{1,0:T(8,128)S(1)}, f32[256,384]{1,0:T(8,128)}, u32[]{:S(2)}) copy-start(f32[256,384]{1,0:T(8,128)} %get-tuple-element.827) | copy-start | bytes 1179652
  634.3 309.3 %all-reduce.49.cloned.1.call-start = ((), (), s32[]{:S(2)}) async-start(), calls=%async_computation.7 | async-start | bytes 3538944 | tf_op jit(solution)/shard_map/psum | solution.py:345
  831.8 139.9 %copy-start.71 = (f32[8,17]{1,0:T(8,128)S(1)}, f32[8,17]{1,0:T(8,128)}, u32[]{:S(2)}) copy-start(f32[8,17]{1,0:T(8,128)} %param.40) | copy-start | bytes 1636
  831.8 142.7 %copy-start.46 = (f32[2,3,48,1536]{3,2,1,0:T(8,128)S(1)}, f32[2,3,48,1536]{3,2,1,0:T(8,128)}, u32[]{:S(2)}) copy-start(f32[2,3,48,1536]{3,2,1,0:T(8,128)} %param.35) | copy-start | bytes 5308420
  832.1 139.6 %copy-start.157 = (f32[8,17]{1,0:T(8,128)S(1)}, f32[8,17]{1,0:T(8,128)}, u32[]{:S(2)}) copy-start(f32[8,17]{1,0:T(8,128)} %param.43) | copy-start | bytes 1636
  832.1 139.6 %copy-start.158 = (f32[8,17]{1,0:T(8,128)S(1)}, f32[8,17]{1,0:T(8,128)}, u32[]{:S(2)}) copy-start(f32[8,17]{1,0:T(8,128)} %param.41) | copy-start | bytes 1636
  (176 other events, 1204.6 us)
Sparse Core Ops, SparseCore 0:
  18.6 22.3 all-gather.9
  43.1 28.5 all-gather.7
  519.1 37.9 reduce-scatter.5
  601.1 230.6 reduce-scatter.7
  835.7 60.1 reduce-scatter.9
  898.3 45.1 all-reduce.48
where the time goes:
time: 996 us; the launch traced here: 989 us
  matrix products  370 us (37%)
  waiting for transfers between devices  301 us (30%)
  local copies, waits for them, and re-layouts  149 us (15%)
  other arithmetic  81.7 us (8%)
  blocking collectives  59.4 us (6%)
  between operations  20.4 us (2%)
    reduce_scatter x1, waiting for transfers between devices, on_device(): lax.psum_scatter(grad_mats, 'dp', scatter_dimension=2, tiled=True)  197 us
    dot_general x33, matrix products, matmul(): jnp.dot(left, right, precision=HIGHEST, preferred_element_type=jnp.float32)  76.3 us
    dot_general x10, matrix products, scores_for(): jnp.einsum('hg,gij->hij', pre_mix, raw_scores, precision=HIGHEST)  69.5 us
    unnamed x7, waiting for transfers between devices  63.6 us
    psum x1, waiting for transfers between devices, on_device(): lax.psum((grad_mats, grad_vecs, grad_talk), 'seq')  34.9 us
    dot_general x10, matrix products, scores_for(): jnp.einsum('ihe,jhe->hij', query_split, keys_split, precision=HIGHEST)  34.9 us
    dot_general x4, matrix products, second_back(): jnp.einsum('hij,gij->hg', d_mixed, raw_scores, precision=HIGHEST)  27 us
    dot_general x6, matrix products, block_tail(): output_rows = jnp.einsum('nf,df->nd', hidden, mats[2], precision=HIGHEST)  26.3 us
  transfers between devices with their start and end apart: 6, of which 4 were waited for; matrix products, arithmetic and copies ran while one was open for 12% of the time, Pallas kernels for 0%

commit v1 on v0

v1 whole, which is shorter than its diff:
```python
import functools

import jax
import jax.numpy as jnp
from jax import lax
from jax.experimental import pallas as pl
from jax.experimental.pallas import tpu as pltpu
from jax.sharding import PartitionSpec as P

STEP = 10
EPS_NORM = 1e-06
MASKED = -1e30
LR_MATRIX = 0.05
LR_VECTOR = 0.1
LR_TALKING = 0.2
BETA_ONE = 0.9
BETA_TWO = 0.999
ADAM_EPS = 1e-08
WEIGHT_DECAY = 0.05
EMA_RATE = 0.9
CLIP_NORM = 1.0
F32 = jnp.float32
BF16 = jnp.bfloat16
NN = (((1,), (0,)), ((), ()))
NT = (((1,), (1,)), ((), ()))
TN = (((0,), (0,)), ((), ()))
VMEM_BYTES = 56 << 20


def split(value):
    high = value.astype(BF16)
    return high, (value - high.astype(F32)).astype(BF16)


def mm(left, right, dims=NN):
    return lax.dot_general(left, right, dims, preferred_element_type=F32)


def mm3(left, right, dims=NN):
    return mm(left[0], right[0], dims) + (mm(left[0], right[1], dims) + mm(left[1], right[0], dims))


def dot_kernel(left, right, dims=NN):
    return mm3(split(left), split(right), dims)


def dot_plain(left, right, dims=NN):
    return lax.dot_general(
        left, right, dims, precision=lax.Precision.HIGH, preferred_element_type=F32
    )


def norm_rows(values):
    average = jnp.mean(values, axis=-1, keepdims=True)
    centered = values - average
    variance = jnp.mean(centered * centered, axis=-1, keepdims=True)
    scale = lax.rsqrt(variance + EPS_NORM)
    return centered * scale, scale


def norm_back(grad, unit, scale):
    inner = jnp.mean(grad * unit, axis=-1, keepdims=True)
    return scale * (grad - jnp.mean(grad, axis=-1, keepdims=True) - unit * inner)


def gelu_both(values):
    half = 0.5 * (1.0 + lax.erf(values * 0.7071067811865476))
    slope = half + values * (0.3989422804014327 * jnp.exp(-0.5 * values * values))
    return values * half, slope


def row_sum(values):
    return jnp.sum(values, axis=0, keepdims=True)


def tail_forward(dot, inputs, attended, w_out, w_up, w_down, vecs, up_bias):
    projected = dot(attended, w_out) + vecs[4:5]
    mixed = inputs + vecs[5:6] * projected
    unit, scale = norm_rows(mixed)
    normed = unit * vecs[6:7] + vecs[7:8]
    hidden, slope = gelu_both(dot(normed, w_up) + up_bias)
    lowered = dot(hidden, w_down, NT) + vecs[12:13]
    out = mixed + vecs[13:14] * lowered
    return out, (projected, unit, scale, normed, hidden, slope, lowered)


def tail_backward(dot, cot, kept, w_out, w_up, w_down, vecs):
    projected, unit, scale, normed, hidden, slope, lowered = kept
    d_lowered = cot * vecs[13:14]
    d_hidden = dot(d_lowered, w_down) * slope
    d_normed = dot(d_hidden, w_up, NT)
    d_mixed = cot + norm_back(d_normed * vecs[6:7], unit, scale)
    d_projected = d_mixed * vecs[5:6]
    d_attended = dot(d_projected, w_out, NT)
    rows = {
        4: row_sum(d_projected),
        5: row_sum(d_mixed * projected),
        6: row_sum(d_normed * unit),
        7: row_sum(d_normed),
        12: row_sum(d_lowered),
        13: row_sum(cot * lowered),
    }
    return d_mixed, d_attended, d_projected, d_hidden, d_lowered, rows, row_sum(d_hidden)


def image_of(lengths_ref, images, positions):
    end = lengths_ref[0, 0]
    inside = (positions >= end).astype(jnp.int32)
    for image in range(1, images):
        end = end + lengths_ref[0, image]
        inside = inside + (positions >= end).astype(jnp.int32)
    return inside


def same_image(lengths_ref, images, place, slots, rows):
    queries = place * rows + lax.broadcasted_iota(jnp.int32, (1, rows), 1)
    query_image = image_of(lengths_ref, images, queries)
    parts = []
    for slot in range(slots):
        keys = jnp.bitwise_xor(place, slot) * rows + lax.broadcasted_iota(jnp.int32, (rows, 1), 0)
        parts.append(image_of(lengths_ref, images, keys) == query_image)
    return parts


def column_of(table, number):
    lanes = lax.broadcasted_iota(jnp.int32, (1, table.shape[1]), 1)
    return jnp.sum(jnp.where(lanes == number, table, 0.0), axis=1, keepdims=True)


def forward_kernel(slots, images, *refs):
    place_ref, lengths_ref = refs[:2]
    token_refs = refs[2 : 2 + slots]
    w_ref, vecs_ref, t1_ref, t2_ref = refs[2 + slots : 6 + slots]
    (
        p_high_ref, p_low_ref, pv_ref, pv_bias_ref, attended_ref, normed_ref,
        kt_high_ref, kt_low_ref, v_high_ref, v_low_ref, query_ref,
        k_high, k_low, vt_high, vt_low, qt, bias, attended_t,
    ) = refs[6 + slots :]
    rows, width = token_refs[0].shape
    head = pl.program_id(0)
    heads = pl.num_programs(0)
    head_size = width // 8

    @pl.when(head == 0)
    def _():
        place = place_ref[0]
        w_kv = split(w_ref[:, width : 3 * width])
        shift = vecs_ref[3:4, :]
        inside = same_image(lengths_ref, images, place, slots, rows)
        for slot in range(slots):
            unit, _ = norm_rows(token_refs[slot][...])
            normed = unit * vecs_ref[0:1, :] + vecs_ref[1:2, :]
            here = pl.ds(slot * rows, rows)
            normed_ref[here, :] = normed
            normed = split(normed)
            both = mm3(normed, w_kv)
            keys, values = both[:, :width], both[:, width:] + shift
            k_high[here, :], k_low[here, :] = split(keys)
            v_high_ref[here, :], v_low_ref[here, :] = split(values)
            kt_high_ref[:, here], kt_low_ref[:, here] = split(keys.T)
            vt_high[:, here], vt_low[:, here] = split(values.T)
            bias[here, :] = jnp.where(inside[slot], 0.0, MASKED)
            if slot == 0:
                query = mm3(normed, split(w_ref[:, :width])) + vecs_ref[2:3, :]
                query = query * head_size ** (-0.5)
                query_ref[...] = query
                qt[...] = query.T

    mixed = mm3((k_high[...], k_low[...]), split(qt[...] * column_of(t1_ref[...], head)))
    mixed = mixed + bias[...]
    exponentials = jnp.exp(mixed - jnp.max(mixed, axis=0, keepdims=True))
    probs = split(exponentials * (1.0 / jnp.sum(exponentials, axis=0, keepdims=True)))
    p_high_ref[0], p_low_ref[0] = probs
    values = mm3((vt_high[...], vt_low[...]), probs)
    pv_ref[0] = values
    term = values * column_of(t2_ref[...], head)

    @pl.when(head == 0)
    def _():
        attended_t[...] = term

    @pl.when(head > 0)
    def _():
        attended_t[...] += term

    @pl.when(head == heads - 1)
    def _():
        inside = jnp.where(bias[...] < 0.0, 0.0, 1.0).astype(BF16)
        summed = mm(vt_high[...], inside) + mm(vt_low[...], inside)
        pv_bias_ref[...] = summed
        attended_ref[...] = (attended_t[...] + summed * t2_ref[:, 8:9]).T


def whole(shape):
    return pl.BlockSpec(shape, lambda *_: (0,) * len(shape))


def struct(shape, dtype=F32):
    return jax.ShapeDtypeStruct(shape, dtype)


def attention_forward(place, lengths, token_slots, w_first, vecs, t1, t2):
    slots, (rows, width) = len(token_slots), token_slots[0].shape
    total, heads = slots * rows, 8
    smem = pl.BlockSpec(memory_space=pltpu.SMEM)
    by_head = lambda *shape: pl.BlockSpec((1,) + shape, lambda g: (g, 0, 0))
    outs = [
        (by_head(total, rows), struct((heads, total, rows), BF16)),
        (by_head(total, rows), struct((heads, total, rows), BF16)),
        (by_head(width, rows), struct((heads, width, rows))),
        (whole((width, rows)), struct((width, rows))),
        (whole((rows, width)), struct((rows, width))),
        (whole((total, width)), struct((total, width))),
        (whole((width, total)), struct((width, total), BF16)),
        (whole((width, total)), struct((width, total), BF16)),
        (whole((total, width)), struct((total, width), BF16)),
        (whole((total, width)), struct((total, width), BF16)),
        (whole((rows, width)), struct((rows, width))),
    ]
    operands = [*token_slots, w_first, vecs, t1, t2]
    flops = 2 * 3 * (2 * heads + 3) * total * rows * width
    return pl.pallas_call(
        functools.partial(forward_kernel, slots, lengths.shape[1]),
        grid=(heads,),
        in_specs=[smem, smem] + [whole(operand.shape) for operand in operands],
        out_specs=[spec for spec, _ in outs],
        out_shape=[shape for _, shape in outs],
        scratch_shapes=[
            pltpu.VMEM((total, width), BF16),
            pltpu.VMEM((total, width), BF16),
            pltpu.VMEM((width, total), BF16),
            pltpu.VMEM((width, total), BF16),
            pltpu.VMEM((width, rows), F32),
            pltpu.VMEM((total, rows), F32),
            pltpu.VMEM((width, rows), F32),
        ],
        compiler_params=pltpu.CompilerParams(vmem_limit_bytes=VMEM_BYTES),
        cost_estimate=pl.CostEstimate(
            flops=flops, bytes_accessed=20 << 20, transcendentals=heads * total * rows
        ),
        name="attention_forward",
    )(place, lengths, *operands)


def backward_kernel(slots, images, *refs):
    (
        place_ref, lengths_ref, p_high_ref, p_low_ref, pv_ref, pv_bias_ref, cot_ref,
        kt_high, kt_low, v_high, v_low, query_ref, t1_ref, t2_ref, t1_rows, t2_rows,
        d_keys_ref, d_values_ref, d_query_ref, c1_ref, c2_ref,
        cot_t, qt, d_qt,
    ) = refs
    rows, width = cot_ref.shape
    head = pl.program_id(0)
    heads = pl.num_programs(0)
    head_size = width // 8
    lanes = lax.broadcasted_iota(jnp.int32, (1, 128), 1)

    @pl.when(head == 0)
    def _():
        cot_t[...] = cot_ref[...].T
        qt[...] = query_ref[...].T
        d_qt[...] = jnp.zeros_like(d_qt)
        d_keys_ref[...] = jnp.zeros_like(d_keys_ref)
        c1_ref[...] = jnp.zeros_like(c1_ref)
        c2_ref[...] = jnp.where(
            lanes == 8, jnp.sum(cot_t[...] * pv_bias_ref[...], axis=1, keepdims=True), 0.0
        )
        inside = jnp.concatenate(same_image(lengths_ref, images, place_ref[0], slots, rows), axis=0)
        inside = jnp.where(inside, 1.0, 0.0).astype(BF16)
        high, low = split(cot_ref[...] * t2_rows[8:9, :])
        d_values_ref[...] = mm(inside, high) + mm(inside, low)

    t1_column = column_of(t1_ref[...], head)
    t2_column = column_of(t2_ref[...], head)
    crossed = cot_t[...] * pv_ref[0]
    c2_ref[...] += jnp.where(lanes == head, jnp.sum(crossed, axis=1, keepdims=True), 0.0)
    delta = jnp.sum(crossed * t2_column, axis=0, keepdims=True)
    d_probs = mm3((v_high[...], v_low[...]), split(cot_t[...] * t2_column))
    probs = (p_high_ref[0], p_low_ref[0])
    d_values_ref[...] += mm3(probs, split(cot_ref[...] * t2_rows[pl.ds(head, 1), :]))
    d_mixed = (probs[0].astype(F32) + probs[1].astype(F32)) * (d_probs - delta)
    d_mixed = split(d_mixed)
    d_keys_ref[...] += mm3(d_mixed, split(query_ref[...] * t1_rows[pl.ds(head, 1), :]))
    back = mm3((kt_high[...], kt_low[...]), d_mixed)
    d_qt[...] += back * t1_column
    c1_ref[...] += jnp.where(
        lanes == head, jnp.sum(back * qt[...], axis=1, keepdims=True), 0.0
    )

    @pl.when(head == heads - 1)
    def _():
        d_query_ref[...] = d_qt[...].T * head_size ** (-0.5)


def attention_backward(place, lengths, p_high, p_low, pv, pv_bias, cot, keys_t, values, query, tables):
    rows, width = cot.shape
    heads, total, _ = p_high.shape
    smem = pl.BlockSpec(memory_space=pltpu.SMEM)
    by_head = lambda shape: pl.BlockSpec((1,) + shape[1:], lambda g: (g, 0, 0))
    operands = [p_high, p_low, pv, pv_bias, cot, *keys_t, *values, query, *tables]
    outs = [struct((total, width)), struct((total, width)), struct((rows, width)),
            struct((width, 128)), struct((width, 128))]
    flops = 2 * 3 * (4 * heads + 1) * total * rows * width
    return pl.pallas_call(
        functools.partial(backward_kernel, total // rows, lengths.shape[1]),
        grid=(heads,),
        in_specs=[smem, smem]
        + [by_head(operand.shape) for operand in operands[:3]]
        + [whole(operand.shape) for operand in operands[3:]],
        out_specs=[whole(out.shape) for out in outs],
        out_shape=outs,
        scratch_shapes=[pltpu.VMEM((width, rows), F32)] * 3,
        compiler_params=pltpu.CompilerParams(vmem_limit_bytes=VMEM_BYTES),
        cost_estimate=pl.CostEstimate(flops=flops, bytes_accessed=20 << 20, transcendentals=0),
        name="attention_backward",
    )(place, lengths, *operands)


def swap(value, axis, size, bit):
    return lax.ppermute(value, axis, [(place, place ^ bit) for place in range(size)])


def gather_slots(own, axis, size):
    found = {0: own}
    bit = size // 2
    while bit:
        for slot in sorted(found):
            found[slot | bit] = swap(found[slot], axis, size, bit)
        bit //= 2
    return [found[slot] for slot in range(size)]


def scatter_slots(parts, axis, size):
    parts = list(parts)
    bit = 1
    while bit < size:
        step = 2 * bit
        for slot in range(0, size, step):
            parts[slot] = parts[slot] + swap(parts[slot + bit], axis, size, bit)
        bit *= 2
    return parts[0]


def reduce_rows(value, dp_size, seq_size):
    dp_index, seq_index = lax.axis_index("dp"), lax.axis_index("seq")
    core = seq_index % 2
    kept = lax.dynamic_index_in_dim(value, core, 1, keepdims=False)
    sent = lax.dynamic_index_in_dim(value, 1 - core, 1, keepdims=False)
    value = kept + swap(sent, "seq", seq_size, 1)
    bit = 1
    while bit < dp_size:
        mine = (dp_index // bit) % 2
        pairs = value.reshape((-1, 2) + value.shape[1:])
        kept = lax.dynamic_index_in_dim(pairs, mine, 1, keepdims=False)
        sent = lax.dynamic_index_in_dim(pairs, 1 - mine, 1, keepdims=False)
        value = kept + swap(sent, "dp", dp_size, bit)
        bit *= 2
    value = value[0]
    bit = 2
    while bit < seq_size:
        value = value + swap(value, "seq", seq_size, bit)
        bit *= 2
    return value


def both_cores(value, seq_size):
    core = lax.axis_index("seq") % 2
    other = swap(value, "seq", seq_size, 1)
    first = jnp.where(core == 0, value, other)
    second = jnp.where(core == 0, other, value)
    return jnp.concatenate([first, second], axis=0)


def adam_step(weight, gradient, moment1, moment2, rate, decay):
    first = BETA_ONE * moment1 + (1.0 - BETA_ONE) * gradient
    second = BETA_TWO * moment2 + (1.0 - BETA_TWO) * gradient * gradient
    first_hat = first / (1.0 - BETA_ONE**STEP)
    second_hat = second / (1.0 - BETA_TWO**STEP)
    updated = weight - rate * (first_hat / (jnp.sqrt(second_hat) + ADAM_EPS) + decay * weight)
    return (updated, first, second)


def on_device(
    dp_size, seq_size,
    tokens, class_tokens, cot_patch, cot_class, lengths,
    matrices, matrices_moment1, matrices_moment2, matrices_ema,
    vectors, vectors_moment1, vectors_moment2, vectors_ema,
    talking, talking_moment1, talking_moment2, talking_ema,
):
    rows, width = tokens.shape
    images = class_tokens.shape[0]
    heads = talking.shape[0]
    head_size = width // heads
    score_scale = head_size ** (-0.5)
    seq_index = lax.axis_index("seq")
    dp_index = lax.axis_index("dp")
    place = seq_index.astype(jnp.int32).reshape(1)
    dot = dot_plain

    mats_self, mats_class = matrices[0], matrices[1]
    vecs_self, vecs_class = vectors[:14], vectors[14:]
    up_bias_self = vecs_self[8:12].reshape(1, -1)
    up_bias_class = vecs_class[8:12].reshape(1, -1)
    pre_mix, post_mix = talking[:, :heads], talking[:, heads:]
    t1 = jnp.repeat(pre_mix.T, head_size, axis=0)
    t2 = jnp.repeat(post_mix, head_size, axis=0)
    tables = (t1, t2, t1.T, t2.T)

    token_slots = gather_slots(tokens, "seq", seq_size)
    (
        p_high, p_low, pv, pv_bias, attended, normed_all,
        kt_high, kt_low, v_high, v_low, query,
    ) = attention_forward(place, lengths, token_slots, mats_self[0], vecs_self, t1, t2)
    self_tail = (mats_self[0][:, 3 * width :], mats_self[1], mats_self[2], vecs_self)
    patch_out, kept_self = tail_forward(dot, tokens, attended, *self_tail, up_bias_self)

    w_q, w_k, w_v, w_o = (mats_class[0][:, i * width : (i + 1) * width] for i in range(4))
    unit_c, scale_c = norm_rows(class_tokens)
    normed_c = unit_c * vecs_class[0:1] + vecs_class[1:2]
    query_c = dot(normed_c, w_q) + vecs_class[2:3]
    keys_c = dot(normed_c, w_k)
    values_c = dot(normed_c, w_v) + vecs_class[3:4]
    heads_of = jnp.arange(width) // head_size
    by_head = (heads_of[None, :] == jnp.arange(heads)[:, None]).astype(F32)

    def spread(value):
        return (value[:, None, :] * by_head[None]).reshape(images * heads, width)

    def gather_heads(value):
        return jnp.sum(value.reshape(images, heads, width) * by_head[None], axis=1)

    def head_sums(value):
        return jnp.sum(spread(value), axis=1, keepdims=True)

    key_rows = dot(spread(query_c), w_k, NT) * score_scale
    own_score = head_sums(query_c * keys_c) * score_scale
    unit_p, scale_p = norm_rows(patch_out)
    normed_p = unit_p * vecs_class[0:1] + vecs_class[1:2]
    ends = jnp.cumsum(lengths[0])
    positions = seq_index * rows + jnp.arange(rows)
    segment = jnp.sum((positions[:, None] >= ends[None, :]).astype(jnp.int32), axis=1)
    belong = jnp.repeat(jnp.arange(images), heads)[:, None] == segment[None, :]
    scores = jnp.where(belong, dot(key_rows, normed_p, NT), MASKED)
    local_top = jnp.max(scores, axis=1, keepdims=True)
    local_weights = jnp.exp(scores - local_top) * belong
    local_sum = jnp.sum(local_weights, axis=1, keepdims=True)
    local_values = dot(local_weights, normed_p)
    packed = jnp.concatenate(
        [local_values, jnp.broadcast_to(local_top, (images * heads, 64)),
         jnp.broadcast_to(local_sum, (images * heads, 64))], axis=1)
    parts = lax.all_gather(packed, "seq", axis=0)
    tops, sums = parts[:, :, width : width + 1], parts[:, :, width + 64 : width + 65]
    class_top = jnp.maximum(jnp.max(tops, axis=0), own_score)
    rescale = jnp.exp(tops - class_top[None])
    own_weight = jnp.exp(own_score - class_top)
    class_sum = jnp.sum(sums * rescale, axis=0) + own_weight
    own_prob = own_weight / class_sum
    normed_rep = jnp.repeat(normed_c, heads, axis=0)
    value_rows = jnp.sum(parts[:, :, :width] * rescale, axis=0) / class_sum + own_prob * normed_rep
    class_attended = gather_heads(dot(value_rows, w_v)) + vecs_class[3:4]
    class_tail = (w_o, mats_class[1], mats_class[2], vecs_class)
    class_out, kept_class = tail_forward(dot, class_tokens, class_attended, *class_tail, up_bias_class)

    grad_class, d_attended_c, d_projected_c, d_hidden_c, d_lowered_c, rows_c, up_c = tail_backward(
        dot, cot_class, kept_class, *class_tail
    )
    class_delta = head_sums(d_attended_c * class_attended)
    cot_rows = dot(spread(d_attended_c), w_v, NT)
    cot_const = head_sums(d_attended_c * vecs_class[3:4])
    probs = jnp.exp(scores - class_top) * belong / class_sum
    d_scores = probs * (dot(cot_rows, normed_p, NT) + cot_const - class_delta)
    d_own = own_prob * (head_sums(d_attended_c * values_c) - class_delta)
    d_normed_p = dot(d_scores, key_rows, TN) + dot(probs, cot_rows, TN)
    d_patch = cot_patch + norm_back(d_normed_p * vecs_class[0:1], unit_p, scale_p)
    rows_p = {0: row_sum(d_normed_p * unit_p), 1: row_sum(d_normed_p)}

    grad_tokens_tail, d_attended, d_projected, d_hidden, d_lowered, rows_s, up_s = tail_backward(
        dot, d_patch, kept_self, *self_tail
    )
    g_out = dot(attended, d_projected, TN)
    g_up = dot(kept_self[3], d_hidden, TN)
    g_down = dot(d_lowered, kept_self[4], TN)

    query_rows = lax.psum(dot(d_scores, normed_p), "seq") + d_own * normed_rep
    d_query_c = gather_heads(dot(query_rows, w_k)) * score_scale
    d_normed_c = dot(d_query_c, w_q, NT) + jnp.sum(
        (d_own * key_rows + own_prob * cot_rows).reshape(images, heads, width), axis=1
    )
    grad_class = grad_class + norm_back(d_normed_c * vecs_class[0:1], unit_c, scale_c)
    rows_c.update({
        0: row_sum(d_normed_c * unit_c), 1: row_sum(d_normed_c),
        2: row_sum(d_query_c), 3: row_sum(d_attended_c),
    })
    factors = jnp.concatenate(
        [normed_c, class_attended, kept_class[3], d_lowered_c, query_rows, value_rows,
         d_query_c, query_c * score_scale, d_attended_c, d_projected_c,
         d_hidden_c.reshape(-1, width), kept_class[4].reshape(-1, width)], axis=0)
    share = factors.shape[0] // seq_size
    factors = lax.dynamic_slice_in_dim(factors, seq_index * share, share, 0)
    factors = lax.all_gather(factors, ("dp", "seq"), axis=0, tiled=True)

    d_keys, d_values, d_query, c1, c2 = attention_backward(
        place, lengths, p_high, p_low, pv, pv_bias, d_attended,
        (kt_high, kt_low), (v_high, v_low), query, tables,
    )
    w_self = mats_self[0]
    d_normed = dot(d_keys, w_self[:, width : 2 * width], NT) + dot(
        d_values, w_self[:, 2 * width : 3 * width], NT
    )
    d_slots = [d_normed[slot * rows : (slot + 1) * rows] for slot in range(seq_size)]
    d_slots[0] = d_slots[0] + dot(d_query, w_self[:, :width], NT)
    d_normed = scatter_slots(d_slots, "seq", seq_size)
    unit_s, scale_s = norm_rows(tokens)
    grad_tokens = grad_tokens_tail + norm_back(d_normed * vecs_self[0:1], unit_s, scale_s)
    rows_s.update({
        0: row_sum(d_normed * unit_s), 1: row_sum(d_normed),
        2: row_sum(d_query), 3: row_sum(d_values),
    })
    g_q = dot(normed_all[:rows], d_query, TN)
    g_k = dot(normed_all, d_keys, TN)
    g_v = dot(normed_all, d_values, TN)

    is_first = (seq_index == 0).astype(F32)

    def vector_rows(found, up):
        named = [found[i] for i in range(8)] + [up.reshape(4, width)] + [found[12], found[13]]
        return jnp.concatenate(named, axis=0)

    found_c = {i: rows_c[i] * is_first for i in rows_c}
    for i in rows_p:
        found_c[i] = found_c[i] + rows_p[i]
    grad_vecs = jnp.concatenate(
        [vector_rows(rows_s, up_s), vector_rows(found_c, up_c * is_first)], axis=0
    )
    fold = lambda value: jnp.sum(value.reshape(heads, head_size, -1), axis=1)
    grad_talk = jnp.concatenate([fold(c1[:, :heads]).T, fold(c2[:, : heads + 1])], axis=1)

    share_rows = width // (2 * dp_size)
    talk_columns = -(-talking.size // share_rows)
    talk_flat = jnp.pad(grad_talk.reshape(-1), (0, talk_columns * share_rows - talking.size))
    talk_block = jnp.tile(talk_flat.reshape(share_rows, talk_columns), (2 * dp_size, 1))
    vec_count = vectors.shape[0]
    spare = 128 - vec_count - talk_columns
    late = jnp.concatenate(
        [g_q, g_k, g_v, grad_vecs.T, talk_block, jnp.zeros((width, spare), F32)], axis=1
    )
    early = jnp.concatenate([g_out, g_up, g_down], axis=1)
    early = reduce_rows(early.reshape(dp_size, 2, share_rows, -1), dp_size, seq_size)
    late = reduce_rows(late.reshape(dp_size, 2, share_rows, -1), dp_size, seq_size)
    grad_talk = late[:, 3 * width + vec_count : 3 * width + vec_count + talk_columns]
    grad_talk = grad_talk.reshape(-1)[: talking.size].reshape(talking.shape)
    late = late[:, : 3 * width + vec_count]

    row_share = width // dp_size
    factors = factors.reshape(dp_size, -1, width)
    mine = lax.dynamic_slice_in_dim(factors, dp_index * row_share, row_share, 2)
    four = lambda array, at, count=images: array[:, at : at + count].reshape(dp_size * count, -1)
    at = images * 4 + 2 * images * heads
    pairs = images * heads

    def headed(left_at, right_at):
        left = mine[:, left_at : left_at + pairs].reshape(-1, heads, row_share)
        right = factors[:, right_at : right_at + images].reshape(-1, heads, head_size)
        out = jnp.einsum("ahr,ahe->rhe", left, right, precision=lax.Precision.HIGH)
        return out.reshape(row_share, width)

    c_first = jnp.concatenate(
        [dot(four(mine, 0), four(factors, at), TN),
         headed(4 * images, at + images),
         headed(4 * images + pairs, at + 2 * images),
         dot(four(mine, images), four(factors, at + 3 * images), TN)], axis=1)
    wide = lambda begin: factors[:, begin : begin + 4 * images].reshape(dp_size * images, 4 * width)
    c_up = dot(four(mine, 2 * images), wide(at + 4 * images), TN)
    c_down = dot(four(mine, 3 * images), wide(at + 8 * images), TN)
    class_share = jnp.stack([c_first, c_up, c_down])

    squares = jnp.sum(early * early) + jnp.sum(late * late) + 0.5 * jnp.sum(class_share * class_share)
    squares = squares.reshape(1, 1)
    squares = squares + swap(squares, "seq", seq_size, 1)
    bit = 1
    while bit < dp_size:
        squares = squares + swap(squares, "dp", dp_size, bit)
        bit *= 2
    clip_norm = jnp.sqrt(squares[0, 0] + jnp.sum(grad_talk * grad_talk))
    factor = jnp.minimum(1.0, CLIP_NORM / clip_norm)
    early = both_cores(early, seq_size)
    late = both_cores(late, seq_size)
    self_share = jnp.stack(
        [jnp.concatenate([late[:, : 3 * width], early[:, :width]], axis=1),
         early[:, width : 5 * width], early[:, 5 * width :]])
    mats_share = jnp.stack([self_share, class_share])
    vecs_share = late[:, 3 * width :].T
    column_share = width // dp_size
    weight_rows = lax.dynamic_slice_in_dim(matrices, dp_index * row_share, row_share, 2)
    vector_columns = lax.dynamic_slice_in_dim(vectors, dp_index * column_share, column_share, 1)
    matrices_new, matrices_first, matrices_second = adam_step(
        weight_rows, mats_share * factor, matrices_moment1, matrices_moment2, LR_MATRIX, WEIGHT_DECAY
    )
    vectors_new, vectors_first, vectors_second = adam_step(
        vector_columns, vecs_share * factor, vectors_moment1, vectors_moment2, LR_VECTOR, 0.0
    )
    talking_new, talking_first, talking_second = adam_step(
        talking, grad_talk * factor, talking_moment1, talking_moment2, LR_TALKING, 0.0
    )
    matrices_average = EMA_RATE * matrices_ema + (1.0 - EMA_RATE) * matrices_new
    vectors_average = EMA_RATE * vectors_ema + (1.0 - EMA_RATE) * vectors_new
    talking_average = EMA_RATE * talking_ema + (1.0 - EMA_RATE) * talking_new
    return (
        patch_out, class_out, grad_tokens, grad_class, clip_norm,
        matrices_new, matrices_first, matrices_second, matrices_average,
        vectors_new, vectors_first, vectors_second, vectors_average,
        talking_new, talking_first, talking_second, talking_average,
    )


def solution(mesh):
    tokens = P(("dp", "seq"), None)
    by_group = P("dp", None)
    mats = P(None, None, "dp", None)
    vecs = P(None, "dp")
    body = functools.partial(on_device, mesh.shape["dp"], mesh.shape["seq"])
    return jax.shard_map(
        body,
        mesh=mesh,
        in_specs=(tokens, by_group, tokens, by_group, by_group, P(), mats, mats, mats,
                  P(), vecs, vecs, vecs, P(), P(), P(), P()),
        out_specs=(tokens, by_group, tokens, by_group, P(), mats, mats, mats, mats,
                   vecs, vecs, vecs, vecs, P(), P(), P(), P()),
        check_vma=False,
    )
```

time: 996 us -> 444 us (0.45)
  matrix products: 370 us -> 72.9 us
  waiting for transfers between devices: 301 us -> 86.8 us
  Pallas kernels: 0 us -> 71.1 us
  local copies, waits for them, and re-layouts: 149 us -> 85.5 us
  blocking collectives: 59.4 us -> 18.3 us
  other arithmetic: 81.7 us -> 56.8 us
  starting transfers between devices: 0.98 us -> 24 us
    dot_general x107 -> x41, matrix products: 370 us -> 72.9 us  [the longest x39 72.2 us: dot_plain(): lax.dot_general(left, right, dims, precision=lax.Precision.HIGH, preferre...]
    reduce_scatter x2 -> x0, waiting for transfers between devices: 197 us -> none  [the longest x1 197 us: on_device(): lax.psum_scatter(grad_mats, 'dp', scatter_dimension=2, tiled=True)]
    pallas_call x0 -> x2, Pallas kernels: none -> 71.1 us  [the longest x1 37.3 us: attention_forward(): pl.pallas_call(functools.partial(forward_kernel, slots, lengths.shape[1])...]
    ppermute x0 -> x22, waiting for transfers between devices: none -> 68.3 us  [swap(): lax.ppermute(value, axis, [(place, place ^ bit) for place in range(size)])]
    unnamed x7 -> x1, waiting for transfers between devices: 63.6 us -> 0.02 us
    psum x1 -> x0, waiting for transfers between devices: 34.9 us -> none  [on_device(): lax.psum((grad_mats, grad_vecs, grad_talk), 'seq')]
    psum x3 -> x1, blocking collectives: 43.8 us -> 12 us  [on_device(): query_rows = lax.psum(dot(d_scores, normed_p), 'seq') + d_own * normed_rep]
    another operation x7 -> x5, other arithmetic: 26.9 us -> 1.17 us  [the longest x2 0.89 us: on_device(): mats_share = jnp.stack([self_share, class_share])]
  transfers between devices with their start and end apart: 6 -> 23, of which waited for: 4 -> 12; matrix products, arithmetic and copies ran while one was open for 12% -> 22% of each run, Pallas kernels for 0% -> 0%
where the time goes in v1:
time: 444 us; the launch traced here: 438 us
  waiting for transfers between devices  86.8 us (20%)
  local copies, waits for them, and re-layouts  85.5 us (19%)
  matrix products  72.9 us (16%)
  Pallas kernels  71.1 us (16%)
  other arithmetic  56.8 us (13%)
  starting transfers between devices  24 us (5%)
  between operations  22.3 us (5%)
  blocking collectives  18.3 us (4%)
    dot_general x39, matrix products, dot_plain(): lax.dot_general(left, right, dims, precision=lax.Precision.HIGH, preferre...  72.2 us
    ppermute x22, waiting for transfers between devices, swap(): lax.ppermute(value, axis, [(place, place ^ bit) for place in range(size)])  68.3 us
    pallas_call x1, Pallas kernels, attention_forward(): pl.pallas_call(functools.partial(forward_kernel, slots, lengths.shape[1])...  37.3 us
    pallas_call x1, Pallas kernels, attention_backward(): pl.pallas_call(functools.partial(backward_kernel, total // rows, lengths....  33.8 us
    ppermute x22, starting transfers between devices, swap(): lax.ppermute(value, axis, [(place, place ^ bit) for place in range(size)])  23.9 us
    unnamed x338, local copies, waits for them, and re-layouts  20.1 us
    all_gather x1, waiting for transfers between devices, on_device(): factors = lax.all_gather(factors, ('dp', 'seq'), axis=0, tiled=True)  18.5 us
    psum x1, blocking collectives, on_device(): query_rows = lax.psum(dot(d_scores, normed_p), 'seq') + d_own * normed_rep  12 us
  transfers between devices with their start and end apart: 23, of which 12 were waited for; matrix products, arithmetic and copies ran while one was open for 22% of the time, Pallas kernels for 0%

profile of v1, /device:TPU:0, one launch (start us, length us, event | category | flops | bytes accessed | tf_op | source)
XLA Modules:
  0.0 437.7 jit_solution(6964703311246372127)
XLA Ops:
  16.5 4.3 slice_bitcast_fusion
  32.1 37.3 %attention_forward.1 = (bf16[8,1024,256]{2,1,0:T(8,128)(2,1)}, bf16[8,1024,256]{2,1,0:T(8,128)(2,1)}, f32[8,384,256]{2,1,0:T(8,128)}, f32[384,256]{1,0:T(8,128)}...) custom-call(s32[1]{0:T(128)} %bitcast.refs_0_, ...), custom_call_target="tpu_custom_call" | custom-call | flops 11475615744 | bytes 20971520 | tf_op jit(solution)/shard_map/attention_forward/pallas_call | solution.py:222
  72.8 3.2 convolution_add_fusion
  76.1 4.5 %fusion.169 = (f32[256]{0:T(256)S(1)}, f32[256,384]{1,0:T(8,128)S(1)}, f32[256,384]{1,0:T(8,128)}) fusion(f32[256,384]{1,0:T(8,128)S(1)} %get-tuple-element.191, f32[384]{0:T(512)S(1)} %copy-done.67, f32[384]{0:T(512)S(1)} %copy-done.117, f32[2,3,384,1536]{3,2,1,0:T(8,128)} %param.22, f32[256,1536]{1,0:T(8,128)S(1)} %convolution_add_fusion), kind=kOutput, calls=%fused_computation.361 | convolution fusion | flops 907935488 | bytes 5115904 | tf_op jit(solution)/shard_map/dot_general | solution.py:48
  82.1 6.3 %all-gather = f32[128,512]{1,0:T(8,128)S(1)} all-gather(f32[32,512]{1,0:T(8,128)S(1)} %pad_maximum_fusion.4), channel_id=2, replica_groups=mesh['dp'=8,'seq'=4] {'seq'}, dimensions={0}, use_global_device_ids=true | all-gather | bytes 327680 | tf_op jit(solution)/shard_map/all_gather | solution.py:451
  111.0 3.3 multiply_reduce_fusion.24
  114.3 3.9 multiply_reduce_fusion.23
  134.4 3.9 fusion.178
  138.3 4.4 %multiply_reduce_fusion.3 = (f32[384]{0:T(512)}, f32[256]{0:T(256)S(1)}, f32[256]{0:T(256)S(1)}, f32[384]{0:T(512)}, f32[256,384]{1,0:T(8,128)S(1)}) fusion(f32[256,384]{1,0:T(8,128)S(1)} %get-tuple-element.191, f32[256]{0:T(256)S(1)} %copy-done.91, f32[256]{0:T(256)S(1)} %copy-done.78, f32[384]{0:T(512)S(1)} %copy-done.71, ...), kind=kOutput, calls=%fused_computation.106 | convolution fusion | flops 906853120 | bytes 4727296 | tf_op jit(solution)/shard_map/dot_general | solution.py:48
  150.4 12.0 %psum.7 = f32[32,384]{1,0:T(8,128)} all-reduce(f32[32,384]{1,0:T(8,128)} %fusion.158), channel_id=1, replica_groups=mesh['dp'=8,'seq'=4] {'seq'}, use_global_device_ids=true, to_apply=%region_29.30 | all-reduce | flops 12288 | bytes 98304 | tf_op jit(solution)/shard_map/psum | solution.py:484
  168.2 33.8 %attention_backward.1 = (f32[1024,384]{1,0:T(8,128)}, f32[1024,384]{1,0:T(8,128)}, f32[256,384]{1,0:T(8,128)}, f32[384,128]{1,0:T(8,128)}, f32[384,128]{1,0:T(8,128)}) custom-call(s32[1]{0:T(128)} %bitcast.refs_0_, s32[1,4]{1,0:T(1,128)} %refs_1_.3, bf16[8,1024,256]{2,1,0:T(8,128)(2,1)} %get-tuple-element.34.refs_2_, ...), custom_call_target="tpu_custom_call" | custom-call | flops 19931332608 | bytes 20971520 | tf_op jit(solution)/shard_map/attention_backward/pallas_call | solution.py:304
  202.0 3.2 fusion.49
  257.0 4.9 %collective-permute-done.5 = f32[256,384]{1,0:T(8,128)} collective-permute-done((f32[256,384]{1,0:T(8,128)}, f32[256,384]{1,0:T(8,128)}, u32[]{:S(2)}, u32[]{:S(2)}) %collective-permute-start.5) | collective-permute-done | bytes 393248 | tf_op jit(solution)/shard_map/ppermute | solution.py:320
  262.0 3.3 multiply_reduce_fusion.5
  266.6 3.9 concatenate.50
  283.6 11.0 %collective-permute-done.12 = f32[4,24,1280]{2,1,0:T(8,128)S(1)} collective-permute-done((f32[4,24,1280]{2,1,0:T(8,128)S(1)}, f32[4,24,1280]{2,1,0:T(8,128)S(1)}, u32[]{:S(2)}, u32[]{:S(2)}) %collective-permute-start.12) | collective-permute-done | bytes 491552 | tf_op jit(solution)/shard_map/ppermute | solution.py:320
  298.1 5.4 %collective-permute-done.13 = f32[2,24,1280]{2,1,0:T(8,128)S(1)} collective-permute-done((f32[2,24,1280]{2,1,0:T(8,128)S(1)}, f32[2,24,1280]{2,1,0:T(8,128)S(1)}, u32[]{:S(2)}, u32[]{:S(2)}) %collective-permute-start.13) | collective-permute-done | bytes 245792 | tf_op jit(solution)/shard_map/ppermute | solution.py:320
  306.4 5.0 %collective-permute-done.14 = f32[1,24,1280]{2,1,0:T(8,128)S(1)} collective-permute-done((f32[1,24,1280]{2,1,0:T(8,128)S(1)}, f32[1,24,1280]{2,1,0:T(8,128)S(1)}, u32[]{:S(2)}, u32[]{:S(2)}) %collective-permute-start.14) | collective-permute-done | bytes 122912 | tf_op jit(solution)/shard_map/ppermute | solution.py:320
  322.6 18.5 %all-gather.3.cloned.1.call-done = f32[1024,384]{1,0:T(8,128)} async-done(((f32[32,384]{1,0:T(8,128)}), f32[1024,384]{1,0:T(8,128)}) %all-gather.3.cloned.1.call-update) | async-done | bytes 1572880 | tf_op jit(solution)/shard_map/all_gather | solution.py:500
  354.0 13.5 %collective-permute-done.8 = f32[2,24,3456]{2,1,0:T(8,128)} collective-permute-done((f32[2,24,3456]{2,1,0:T(8,128)S(1)}, f32[2,24,3456]{2,1,0:T(8,128)}, u32[]{:S(2)}, u32[]{:S(2)}) %collective-permute-start.8) | collective-permute-done | bytes 663584 | tf_op jit(solution)/shard_map/ppermute | solution.py:320
  370.7 13.7 %collective-permute-done.9 = f32[1,24,3456]{2,1,0:T(8,128)S(1)} collective-permute-done((f32[1,24,3456]{2,1,0:T(8,128)S(1)}, f32[1,24,3456]{2,1,0:T(8,128)S(1)}, u32[]{:S(2)}, u32[]{:S(2)}) %collective-permute-start.9) | collective-permute-done | bytes 331808 | tf_op jit(solution)/shard_map/ppermute | solution.py:320
  387.4 6.4 %collective-permute-done.10 = f32[24,3456]{1,0:T(8,128)S(1)} collective-permute-done((f32[24,3456]{1,0:T(8,128)S(1)}, f32[24,3456]{1,0:T(8,128)S(1)}, u32[]{:S(2)}, u32[]{:S(2)}) %collective-permute-start.10) | collective-permute-done | bytes 331808 | tf_op jit(solution)/shard_map/ppermute | solution.py:320
  407.9 3.2 collective-permute-done.19
  423.9 5.7 %multiply_add_fusion = (f32[2,3,48,1536]{3,2,1,0:T(8,128)}, f32[2,3,48,1536]{3,2,1,0:T(8,128)}, f32[2,3,48,1536]{3,2,1,0:T(8,128)}, f32[2,3,48,1536]{3,2,1,0:T(8,128)}) fusion(f32[2,3,48,1536]{3,2,1,0:T(8,128)S(1)} %copy-done.22, f32[2,3,384,1536]{3,2,1,0:T(8,128)} %param.22, s32[]{:T(128)S(6)} %select_n.158, f32[]{:T(128)S(6)} %min.3, ...), kind=kLoop, calls=%fused_computation.37 | loop fusion | flops 8847360 | bytes 15925256 | tf_op jit(solution)/shard_map/add | solution.py:605
  (580 shorter events, 200.7 us)
Async XLA Ops:
  7.2 333.9 %all-gather.3.cloned.1.call-start = ((), (), s32[]{:S(2)}) async-start(), calls=%async_computation | async-start | bytes 1622016 | tf_op jit(solution)/shard_map/all_gather | solution.py:500
  7.2 15.6 %collective-permute-start.1 = (f32[256,384]{1,0:T(8,128)}, f32[256,384]{1,0:T(8,128)S(1)}, u32[]{:S(2)}, u32[]{:S(2)}) collective-permute-start(f32[256,384]{1,0:T(8,128)} %refs_2_.1), channel_id=1, source_target_pairs={{0,2},{1,3},{2,0},{3,1},{4,6},{5,7},{6,4},{7,5},{8,10},{9,11},{10,... | collective-permute-start | bytes 1179656 | tf_op jit(solution)/shard_map/ppermute | solution.py:320
  10.3 21.8 %collective-permute-start = (f32[256,384]{1,0:T(8,128)}, f32[256,384]{1,0:T(8,128)}, u32[]{:S(2)}, u32[]{:S(2)}) collective-permute-start(f32[256,384]{1,0:T(8,128)} %refs_2_.1), channel_id=1, source_target_pairs={{0,1},{1,0},{2,3},{3,2},{4,5},{5,4},{6,7},{7,6},{8,9},{9,8},{10,11... | collective-permute-start | bytes 1179656 | tf_op jit(solution)/shard_map/ppermute | solution.py:320
  15.6 57.1 %copy-start.103 = (f32[384]{0:T(512)}, f32[384]{0:T(512)S(1)}, u32[]{:S(2)}) copy-start(f32[384]{0:T(512)S(1)} %get-tuple-element.145) | copy-start | bytes 4612
  22.9 9.2 %collective-permute-start.2 = (f32[256,384]{1,0:T(8,128)S(1)}, f32[256,384]{1,0:T(8,128)}, u32[]{:S(2)}, u32[]{:S(2)}) collective-permute-start(f32[256,384]{1,0:T(8,128)S(1)} %collective-permute-done.1.refs_4_), channel_id=1, source_target_pairs={{0,1},{1,0},{2,3},{3,2},{4,5},{5,4},{6,7},{7,6},{8,9},{9,8},{10,11... | collective-permute-start | bytes 1179656 | tf_op jit(solution)/shard_map/ppermute | solution.py:320
  214.9 33.8 %collective-permute-start.4 = (f32[256,384]{1,0:T(8,128)}, f32[256,384]{1,0:T(8,128)}, u32[]{:S(2)}, u32[]{:S(2)}) collective-permute-start(f32[256,384]{1,0:T(8,128)} %get-tuple-element.207), channel_id=1, source_target_pairs={{0,1},{1,0},{2,3},{3,2},{4,5},{5,4},{6,7},{7,6},{8,9},{9,8},{10,11... | collective-permute-start | bytes 1179656 | tf_op jit(solution)/shard_map/ppermute | solution.py:320
  245.5 11.6 %collective-permute-start.3 = (f32[256,384]{1,0:T(8,128)}, f32[256,384]{1,0:T(8,128)}, u32[]{:S(2)}, u32[]{:S(2)}) collective-permute-start(f32[256,384]{1,0:T(8,128)} %get-tuple-element.206), channel_id=1, source_target_pairs={{0,1},{1,0},{2,3},{3,2},{4,5},{5,4},{6,7},{7,6},{8,9},{9,8},{10,11... | collective-permute-start | bytes 1179656 | tf_op jit(solution)/shard_map/ppermute | solution.py:320
  250.5 11.4 %collective-permute-start.5 = (f32[256,384]{1,0:T(8,128)}, f32[256,384]{1,0:T(8,128)}, u32[]{:S(2)}, u32[]{:S(2)}) collective-permute-start(f32[256,384]{1,0:T(8,128)} %slice_add_fusion), channel_id=1, source_target_pairs={{0,2},{1,3},{2,0},{3,1},{4,6},{5,7},{6,4},{7,5},{8,10},{9,11},{10,... | collective-permute-start | bytes 1179656 | tf_op jit(solution)/shard_map/ppermute | solution.py:320
  272.8 6.2 %collective-permute-start.11 = (f32[8,24,1280]{2,1,0:T(8,128)}, f32[8,24,1280]{2,1,0:T(8,128)}, u32[]{:S(2)}, u32[]{:S(2)}) collective-permute-start(f32[8,24,1280]{2,1,0:T(8,128)} %dynamic-slice_bitcast_fusion.2), channel_id=1, source_target_pairs={{0,1},{1,0},{2,3},{3,2},{4,5},{5,4},{6,7},{7,6},{8,9},{9,8},{10,11... | collective-permute-start | bytes 2949128 | tf_op jit(solution)/shard_map/ppermute | solution.py:320
  278.3 34.3 %collective-permute-start.6 = (f32[8,24,3456]{2,1,0:T(8,128)}, f32[8,24,3456]{2,1,0:T(8,128)}, u32[]{:S(2)}, u32[]{:S(2)}) collective-permute-start(f32[8,24,3456]{2,1,0:T(8,128)} %dynamic-slice_bitcast_fusion), channel_id=1, source_target_pairs={{0,1},{1,0},{2,3},{3,2},{4,5},{5,4},{6,7},{7,6},{8,9},{9,8},{10,11... | collective-permute-start | bytes 7962632 | tf_op jit(solution)/shard_map/ppermute | solution.py:320
  281.4 13.3 %collective-permute-start.12 = (f32[4,24,1280]{2,1,0:T(8,128)S(1)}, f32[4,24,1280]{2,1,0:T(8,128)S(1)}, u32[]{:S(2)}, u32[]{:S(2)}) collective-permute-start(f32[4,24,1280]{2,1,0:T(8,128)S(1)} %dynamic-slice_bitcast_fusion.4), channel_id=1, source_target_pairs={{0,4},{4,0},{8,12},{12,8},{16,20},{20,16},{24,28},{28,24},{1,5},{5... | collective-permute-start | bytes 1474568 | tf_op jit(solution)/shard_map/ppermute | solution.py:320
  295.7 7.7 %collective-permute-start.13 = (f32[2,24,1280]{2,1,0:T(8,128)S(1)}, f32[2,24,1280]{2,1,0:T(8,128)S(1)}, u32[]{:S(2)}, u32[]{:S(2)}) collective-permute-start(f32[2,24,1280]{2,1,0:T(8,128)S(1)} %dynamic-slice_bitcast_fusion.5), channel_id=1, source_target_pairs={{0,8},{4,12},{8,0},{12,4},{16,24},{20,28},{24,16},{28,20},{1,9},{5... | collective-permute-start | bytes 737288 | tf_op jit(solution)/shard_map/ppermute | solution.py:320
  303.5 7.9 %collective-permute-start.14 = (f32[1,24,1280]{2,1,0:T(8,128)S(1)}, f32[1,24,1280]{2,1,0:T(8,128)S(1)}, u32[]{:S(2)}, u32[]{:S(2)}) collective-permute-start(f32[1,24,1280]{2,1,0:T(8,128)S(1)} %constant_dynamic-slice_fusion.8), channel_id=1, source_target_pairs={{0,16},{4,20},{8,24},{12,28},{16,0},{20,4},{24,8},{28,12},{1,17},{... | collective-permute-start | bytes 368648 | tf_op jit(solution)/shard_map/ppermute | solution.py:320
  311.4 6.4 %collective-permute-start.15 = (f32[24,1280]{1,0:T(8,128)S(1)}, f32[24,1280]{1,0:T(8,128)S(1)}, u32[]{:S(2)}, u32[]{:S(2)}) collective-permute-start(f32[24,1280]{1,0:T(8,128)S(1)} %add_bitcast_fusion.1), channel_id=1, source_target_pairs={{0,2},{1,3},{2,0},{3,1},{4,6},{5,7},{6,4},{7,5},{8,10},{9,11},{10,... | collective-permute-start | bytes 368648 | tf_op jit(solution)/shard_map/ppermute | solution.py:320
  316.6 32.4 %collective-permute-start.7 = (f32[4,24,3456]{2,1,0:T(8,128)}, f32[4,24,3456]{2,1,0:T(8,128)}, u32[]{:S(2)}, u32[]{:S(2)}) collective-permute-start(f32[4,24,3456]{2,1,0:T(8,128)} %dynamic-slice_bitcast_fusion.1), channel_id=1, source_target_pairs={{0,4},{4,0},{8,12},{12,8},{16,20},{20,16},{24,28},{28,24},{1,5},{5... | collective-permute-start | bytes 3981320 | tf_op jit(solution)/shard_map/ppermute | solution.py:320
  318.5 2.5 collective-permute-start.20
  351.7 15.9 %collective-permute-start.8 = (f32[2,24,3456]{2,1,0:T(8,128)S(1)}, f32[2,24,3456]{2,1,0:T(8,128)}, u32[]{:S(2)}, u32[]{:S(2)}) collective-permute-start(f32[2,24,3456]{2,1,0:T(8,128)S(1)} %dynamic-slice_bitcast_fusion.3), channel_id=1, source_target_pairs={{0,8},{4,12},{8,0},{12,4},{16,24},{20,28},{24,16},{28,20},{1,9},{5... | collective-permute-start | bytes 1990664 | tf_op jit(solution)/shard_map/ppermute | solution.py:320
  368.7 15.8 %collective-permute-start.9 = (f32[1,24,3456]{2,1,0:T(8,128)S(1)}, f32[1,24,3456]{2,1,0:T(8,128)S(1)}, u32[]{:S(2)}, u32[]{:S(2)}) collective-permute-start(f32[1,24,3456]{2,1,0:T(8,128)S(1)} %constant_dynamic-slice_fusion.9), channel_id=1, source_target_pairs={{0,16},{4,20},{8,24},{12,28},{16,0},{20,4},{24,8},{28,12},{1,17},{... | collective-permute-start | bytes 995336 | tf_op jit(solution)/shard_map/ppermute | solution.py:320
  384.6 9.2 %collective-permute-start.10 = (f32[24,3456]{1,0:T(8,128)S(1)}, f32[24,3456]{1,0:T(8,128)S(1)}, u32[]{:S(2)}, u32[]{:S(2)}) collective-permute-start(f32[24,3456]{1,0:T(8,128)S(1)} %add_bitcast_fusion), channel_id=1, source_target_pairs={{0,2},{1,3},{2,0},{3,1},{4,6},{5,7},{6,4},{7,5},{8,10},{9,11},{10,... | collective-permute-start | bytes 995336 | tf_op jit(solution)/shard_map/ppermute | solution.py:320
  395.8 1.5 collective-permute-start.16
  396.8 24.0 %collective-permute-start.21 = (f32[24,3456]{1,0:T(8,128)S(1)}, f32[24,3456]{1,0:T(8,128)}, u32[]{:S(2)}, u32[]{:S(2)}) collective-permute-start(f32[24,3456]{1,0:T(8,128)S(1)} %get-tuple-element.182), channel_id=1, source_target_pairs={{0,1},{1,0},{2,3},{3,2},{4,5},{5,4},{6,7},{7,6},{8,9},{9,8},{10,11... | collective-permute-start | bytes 995336 | tf_op jit(solution)/shard_map/ppermute | solution.py:320
  397.9 3.7 collective-permute-start.17
  402.2 3.7 collective-permute-start.18
  406.4 4.6 %collective-permute-start.19 = (f32[1,1]{1,0:T(1,128)}, f32[1,1]{1,0:T(1,128)}, u32[]{:S(2)}, u32[]{:S(2)}) collective-permute-start(f32[1,1]{1,0:T(1,128)} %add.602), channel_id=1, source_target_pairs={{0,16},{4,20},{8,24},{12,28},{16,0},{20,4},{24,8},{28,12},{1,17},{... | collective-permute-start | bytes 20 | tf_op jit(solution)/shard_map/ppermute | solution.py:320
  (163 other events, 1666.2 us)
Sparse Core Ops, SparseCore 0:
  283.7 57.3 all-gather.2
